TPU v7x, 32 devices: a whole 2x2x4 slice. The times are simulated.
32 devices in a mesh: context: 4 (over z), mirror: 2 (over core), tensor: 4 (over y, x).
Axes of the slice: x: 2, y: 2, z: 4, core: 2. Of those that a mesh axis runs over, the one named last changes fastest.
Arguments:
- hyena_q: bfloat16 [1024, 8192], P(('context', 'mirror'), 'tensor'), may hold values from -57 to 57
- hyena_k: bfloat16 [1024, 8192], P(('context', 'mirror'), 'tensor'), may hold values from -6 to 6
- hyena_v: bfloat16 [1024, 8192], P(('context', 'mirror'), 'tensor'), may hold values from -6 to 6
- filters: bfloat16 [512, 128], P('tensor'), may hold values from -0.5 to 0.5
- norm_gain: float32 [8192], P('tensor'), may hold values from 0.1 to 1.9
- attn_q: bfloat16 [1024, 8192], P(('context', 'mirror'), 'tensor'), may hold values from -35 to 35
- attn_k: bfloat16 [1024, 8192], P(('context', 'mirror'), 'tensor'), may hold values from -5 to 5
- out_grad: bfloat16 [1024, 8192], P(('context', 'mirror'), 'tensor'), may hold values from -20 to 20
- doc_lengths: int32 [4], replicated, may hold values from 1 to 512, 1024 in all
Outputs:
- attn_out: bfloat16 [1024, 8192], P(('context', 'mirror'), 'tensor')
- grad_attn_q: bfloat16 [1024, 8192], P(('context', 'mirror'), 'tensor')
- grad_attn_k: bfloat16 [1024, 8192], P(('context', 'mirror'), 'tensor')
- grad_hyena_q: bfloat16 [1024, 8192], P(('context', 'mirror'), 'tensor')
- grad_hyena_k: bfloat16 [1024, 8192], P(('context', 'mirror'), 'tensor')
- grad_hyena_v: bfloat16 [1024, 8192], P(('context', 'mirror'), 'tensor')
- grad_filters: float32 [512, 128], P('tensor')
All inputs are finite; a program needn't handle non-finite values.
Results may differ from a plain program's by a relative error of at most 0.0064.
Values may be sent and summed in bfloat16 or wider, within the bound.
A program may use at most 128 MiB of HBM per device.

v0:
```python
import jax
import jax.numpy as jnp
from jax import lax
from jax.sharding import PartitionSpec as P

HEAD = 128
D = 8192
REACH = 2


def passed_along(block, axis, distance):
    devices = range(lax.axis_size(axis))
    route = [(i - distance, i) for i in devices if i - distance in devices]
    return lax.ppermute(block, axis, route)


def doc_index(doc_lengths, positions):
    doc_ends = jnp.cumsum(doc_lengths, dtype=jnp.int32)
    return jnp.sum(
        (positions[:, None] >= doc_ends[None, :]).astype(jnp.int32), axis=1, dtype=jnp.int32
    )


def banded(band_table, row_count, col_count):
    repeated = jnp.tile(band_table, (1, row_count + 1))[:, : row_count * col_count]
    return repeated.reshape(band_table.shape[0], row_count, col_count)


def attend(queries, key_heads, allowed, score_scale):
    scores = (
        jnp.einsum("thd,uhd->htu", queries, key_heads, preferred_element_type=jnp.float32)
        * score_scale
    )
    row_top = jnp.max(jnp.where(allowed[None], scores, -1e30), axis=2, keepdims=True)
    row_total = jnp.sum(
        jnp.exp(jnp.where(allowed[None], scores - row_top, -1e30)), axis=2, keepdims=True
    )
    row_lse = row_top + jnp.log(row_total)
    return (jnp.where(allowed[None], jnp.exp(scores - row_lse), 0.0), row_lse)


def body(hyena_q, hyena_k, hyena_v, filters, norm_gain, attn_q, attn_k, out_grad, doc_lengths):
    tok_rows, channels = hyena_q.shape
    groups, tap_count = filters.shape
    group_width = channels // groups
    heads_dev = channels // HEAD
    pad_rows = tok_rows + tap_count
    offset = lax.axis_index(("context", "mirror")) * tok_rows
    score_scale = HEAD ** (-0.5)
    window_span = REACH * tok_rows
    own_pos = offset + jnp.arange(tok_rows, dtype=jnp.int32)
    own_doc = doc_index(doc_lengths, own_pos)
    kv_product = (hyena_k.astype(jnp.float32) * hyena_v.astype(jnp.float32)).astype(jnp.bfloat16)
    left_rim = passed_along(kv_product[tok_rows - (tap_count - 1) :], ("context", "mirror"), 1)
    wide_pad = jnp.concatenate(
        [left_rim, kv_product, jnp.zeros((1, channels), jnp.bfloat16)], axis=0
    )
    wide_pos = offset - (tap_count - 1) + jnp.arange(pad_rows, dtype=jnp.int32)
    fwd_mask = own_doc[:, None] == doc_index(doc_lengths, wide_pos)[None, :]
    zeros_tail = jnp.zeros((groups, pad_rows + 1 - tap_count), jnp.bfloat16)
    fwd_table = jnp.concatenate([filters[:, ::-1], zeros_tail], axis=1)
    fwd_band = banded(fwd_table, tok_rows, pad_rows) * fwd_mask[None].astype(jnp.bfloat16)
    wide_groups = wide_pad.reshape(pad_rows, groups, group_width)
    signal = jnp.einsum(
        "gtu,ugc->tgc", fwd_band, wide_groups, preferred_element_type=jnp.float32
    ).reshape(tok_rows, channels)
    hyena_mix = hyena_q.astype(jnp.float32) * signal
    square_sum = lax.psum(jnp.sum(hyena_mix * hyena_mix, axis=1), "tensor")
    inv_rms = lax.rsqrt(square_sum / D + 1e-06)
    values = (hyena_mix * inv_rms[:, None] * norm_gain[None, :]).astype(jnp.bfloat16)
    earlier = []
    for distance in range(1, REACH + 1):
        earlier.append(passed_along((attn_k, values), ("context", "mirror"), distance))
    key_win = jnp.concatenate([piece[0] for piece in earlier[::-1]] + [attn_k], axis=0)
    value_win = jnp.concatenate([piece[1] for piece in earlier[::-1]] + [values], axis=0)
    window = (REACH + 1) * tok_rows
    key_pos = offset - REACH * tok_rows + jnp.arange(window, dtype=jnp.int32)
    key_doc = doc_index(doc_lengths, key_pos)
    allowed = (
        (key_pos[None, :] >= 0)
        & (key_pos[None, :] <= own_pos[:, None])
        & (own_pos[:, None] - key_pos[None, :] <= window_span)
        & (key_doc[None, :] == own_doc[:, None])
    )
    queries = attn_q.reshape(tok_rows, heads_dev, HEAD)
    grad_heads = out_grad.reshape(tok_rows, heads_dev, HEAD)
    key_heads = key_win.reshape(window, heads_dev, HEAD)
    value_heads = value_win.reshape(window, heads_dev, HEAD)
    attn_prob, row_lse = attend(queries, key_heads, allowed, score_scale)
    prob_half = attn_prob.astype(jnp.bfloat16)
    attn_out = (
        jnp.einsum("htu,uhd->thd", prob_half, value_heads, preferred_element_type=jnp.float32)
        .astype(jnp.bfloat16)
        .reshape(tok_rows, channels)
    )
    grad_prob = jnp.einsum(
        "thd,uhd->htu", grad_heads, value_heads, preferred_element_type=jnp.float32
    )
    row_delta = jnp.sum(attn_prob * grad_prob, axis=2, keepdims=True)
    grad_score = (attn_prob * (grad_prob - row_delta) * score_scale).astype(jnp.bfloat16)
    grad_attn_q = (
        jnp.einsum("htu,uhd->thd", grad_score, key_heads, preferred_element_type=jnp.float32)
        .astype(jnp.bfloat16)
        .reshape(tok_rows, channels)
    )
    own_start = REACH * tok_rows
    key_part = jnp.einsum("htu,thd->uhd", grad_score, queries, preferred_element_type=jnp.float32)
    value_part = jnp.einsum(
        "htu,thd->uhd", prob_half, grad_heads, preferred_element_type=jnp.float32
    )
    grad_keys = key_part[own_start:]
    grad_vals = value_part[own_start:]
    for distance in range(1, REACH + 1):
        low_row = (REACH - distance) * tok_rows
        returned = passed_along(
            (key_part[low_row : low_row + tok_rows], value_part[low_row : low_row + tok_rows]),
            ("context", "mirror"),
            -distance,
        )
        grad_keys = grad_keys + returned[0]
        grad_vals = grad_vals + returned[1]
    grad_attn_k = grad_keys.astype(jnp.bfloat16).reshape(tok_rows, channels)
    grad_values = grad_vals.reshape(tok_rows, channels)
    inner_sum = lax.psum(jnp.sum(norm_gain[None, :] * grad_values * hyena_mix, axis=1), "tensor")
    grad_mix = inv_rms[:, None] * (
        norm_gain[None, :] * grad_values - hyena_mix * (inner_sum * inv_rms * inv_rms / D)[:, None]
    )
    grad_hyena_q = (grad_mix * signal).astype(jnp.bfloat16)
    grad_signal = (grad_mix * hyena_q.astype(jnp.float32)).astype(jnp.bfloat16)
    right_rim = passed_along(grad_signal[: tap_count - 1], ("context", "mirror"), -1)
    back_pad = jnp.concatenate(
        [grad_signal, right_rim, jnp.zeros((1, channels), jnp.bfloat16)], axis=0
    )
    back_pos = offset + jnp.arange(pad_rows, dtype=jnp.int32)
    back_mask = own_doc[:, None] == doc_index(doc_lengths, back_pos)[None, :]
    back_table = jnp.concatenate([filters, zeros_tail], axis=1)
    back_band = banded(back_table, tok_rows, pad_rows) * back_mask[None].astype(jnp.bfloat16)
    grad_kv = jnp.einsum(
        "gtu,ugc->tgc",
        back_band,
        back_pad.reshape(pad_rows, groups, group_width),
        preferred_element_type=jnp.float32,
    ).reshape(tok_rows, channels)
    grad_hyena_k = (grad_kv * hyena_v.astype(jnp.float32)).astype(jnp.bfloat16)
    grad_hyena_v = (grad_kv * hyena_k.astype(jnp.float32)).astype(jnp.bfloat16)
    block_count = 4
    block_size = groups // block_count
    mask_float = fwd_mask.astype(jnp.float32)

    def filter_block(pieces):
        grad_block, wide_block = pieces
        correlation = (
            jnp.einsum("tgc,ugc->gtu", grad_block, wide_block, preferred_element_type=jnp.float32)
            * mask_float[None]
        )
        flattened = jnp.pad(
            correlation.reshape(block_size, tok_rows * pad_rows), ((0, 0), (0, tok_rows))
        )
        diagonal = flattened.reshape(block_size, tok_rows, pad_rows + 1)[:, :, :tap_count]
        return jnp.sum(diagonal, axis=1)[:, ::-1]

    grad_blocks = grad_signal.reshape(tok_rows, block_count, block_size, group_width).transpose(
        1, 0, 2, 3
    )
    wide_blocks = wide_groups.reshape(pad_rows, block_count, block_size, group_width).transpose(
        1, 0, 2, 3
    )
    local_filters = lax.map(filter_block, (grad_blocks, wide_blocks)).reshape(groups, tap_count)
    grad_filters = lax.psum(local_filters, ("context", "mirror"))
    return (
        attn_out,
        grad_attn_q,
        grad_attn_k,
        grad_hyena_q,
        grad_hyena_k,
        grad_hyena_v,
        grad_filters,
    )


def solution(mesh):
    return jax.shard_map(
        body,
        mesh=mesh,
        in_specs=(
            P(("context", "mirror"), "tensor"),
            P(("context", "mirror"), "tensor"),
            P(("context", "mirror"), "tensor"),
            P("tensor", None),
            P("tensor"),
            P(("context", "mirror"), "tensor"),
            P(("context", "mirror"), "tensor"),
            P(("context", "mirror"), "tensor"),
            P(),
        ),
        out_specs=(
            P(("context", "mirror"), "tensor"),
            P(("context", "mirror"), "tensor"),
            P(("context", "mirror"), "tensor"),
            P(("context", "mirror"), "tensor"),
            P(("context", "mirror"), "tensor"),
            P(("context", "mirror"), "tensor"),
            P("tensor", None),
        ),
        check_vma=False,
    )
```

profile of v0, /device:TPU:1, one launch (start us, length us, event | category | flops | bytes accessed | tf_op | source)
XLA Modules:
  0.0 310.3 jit_solution(5545517757831475198)
XLA Ops:
  7.2 1.4 copy.70
  8.6 4.7 %collective-permute-start.4 = (bf16[128,2048]{0,1:T(8,128)(2,1)S(1)}, bf16[128,2048]{0,1:T(8,128)(2,1)}, u32[]{:S(2)}, u32[]{:S(2)}) collective-permute-start(bf16[128,2048]{0,1:T(8,128)(2,1)S(1)} %copy.70), channel_id=1, source_target_pairs={{0,4},{4,8},{8,12},{12,16},{16,20},{20,24},{24,28},{1,5},{5,9},{9,... | collective-permute-start | bytes 1572872 | tf_op jit(solution)/shard_map/ppermute | solution.py:14
  13.3 4.0 %collective-permute-start.3 = (bf16[128,2048]{0,1:T(8,128)(2,1)S(1)}, bf16[128,2048]{0,1:T(8,128)(2,1)}, u32[]{:S(2)}, u32[]{:S(2)}) collective-permute-start(bf16[128,2048]{0,1:T(8,128)(2,1)S(1)} %copy.70), channel_id=1, source_target_pairs={{0,8},{4,12},{8,16},{12,20},{16,24},{20,28},{1,9},{5,13},{9,17},{1... | collective-permute-start | bytes 1572872 | tf_op jit(solution)/shard_map/ppermute | solution.py:14
  18.7 1.5 copy.66
  22.2 1.9 collective-permute-start
  27.9 4.5 %tile.8 = bf16[128,129,257]{0,2,1:T(8,128)(2,1)} broadcast(bf16[128,257]{0,1:T(8,128)(2,1)S(1)} %concatenate.19.clone), dimensions={0,2} | broadcast | bytes 8552960 | tf_op jit(solution)/shard_map/tile | solution.py:25
  32.4 13.2 %tile.9 = bf16[128,33153]{0,1:T(8,128)(2,1)} reshape(bf16[128,129,257]{0,2,1:T(8,128)(2,1)} %tile.8) | data formatting | bytes 16974336 | tf_op jit(solution)/shard_map/tile | solution.py:25
  45.6 7.1 %slice.49 = bf16[128,32768]{0,1:T(8,128)(2,1)} slice(bf16[128,33153]{0,1:T(8,128)(2,1)} %tile.9), slice={[0:128], [0:32768]} | slice | bytes 16777216 | tf_op jit(solution)/shard_map/slice | solution.py:25
  52.7 12.5 %copy.69 = bf16[128,128,256]{2,1,0:T(8,128)(2,1)} copy(bf16[128,128,256]{0,2,1:T(8,128)(2,1)} %bitcast.165) | data formatting | bytes 16777216 | tf_op jit(solution)/shard_map/reshape | solution.py:26
  65.1 4.5 %tile.20 = bf16[128,129,257]{0,2,1:T(8,128)(2,1)} broadcast(bf16[128,257]{0,1:T(8,128)(2,1)S(1)} %concatenate.23.clone), dimensions={0,2} | broadcast | bytes 8552960 | tf_op jit(solution)/shard_map/tile | solution.py:25
  69.6 13.2 %tile.21 = bf16[128,33153]{0,1:T(8,128)(2,1)} reshape(bf16[128,129,257]{0,2,1:T(8,128)(2,1)} %tile.20) | data formatting | bytes 16974336 | tf_op jit(solution)/shard_map/tile | solution.py:25
  82.8 7.1 %slice.57 = bf16[128,32768]{0,1:T(8,128)(2,1)} slice(bf16[128,33153]{0,1:T(8,128)(2,1)} %tile.21), slice={[0:128], [0:32768]} | slice | bytes 16777216 | tf_op jit(solution)/shard_map/slice | solution.py:25
  89.9 12.6 %copy.84 = bf16[128,128,256]{2,1,0:T(8,128)(2,1)} copy(bf16[128,128,256]{0,2,1:T(8,128)(2,1)} %bitcast.166) | data formatting | bytes 16777216 | tf_op jit(solution)/shard_map/reshape | solution.py:26
  103.0 1.4 pad_maximum_fusion.1
  107.0 1.6 collective-permute-start.8
  108.6 3.4 %collective-permute-start.7 = (f32[128,16,128]{0,2,1:T(8,128)S(1)}, f32[128,16,128]{0,2,1:T(8,128)S(1)}, u32[]{:S(2)}, u32[]{:S(2)}) collective-permute-start(f32[128,16,128]{0,2,1:T(8,128)S(1)} %get-tuple-element.130), channel_id=1, source_target_pairs={{4,0},{8,4},{12,8},{16,12},{20,16},{24,20},{28,24},{5,1},{9,5},{13... | collective-permute-start | bytes 3145736 | tf_op jit(solution)/shard_map/ppermute | solution.py:14
  112.0 1.5 maximum_maximum_fusion
  113.6 2.3 fusion.10
  115.9 16.7 %collective-permute-done.8 = f32[128,16,128]{0,2,1:T(8,128)S(1)} collective-permute-done((f32[128,16,128]{0,2,1:T(8,128)S(1)}, f32[128,16,128]{0,2,1:T(8,128)S(1)}, u32[]{:S(2)}, u32[]{:S(2)}) %collective-permute-start.8) | collective-permute-done | bytes 1048608 | tf_op jit(solution)/shard_map/ppermute | solution.py:14
  132.6 12.8 %collective-permute-done.7 = f32[128,16,128]{0,2,1:T(8,128)S(1)} collective-permute-done((f32[128,16,128]{0,2,1:T(8,128)S(1)}, f32[128,16,128]{0,2,1:T(8,128)S(1)}, u32[]{:S(2)}, u32[]{:S(2)}) %collective-permute-start.7) | collective-permute-done | bytes 1048608 | tf_op jit(solution)/shard_map/ppermute | solution.py:14
  146.6 7.8 %all-reduce.3 = (f32[128]{0:T(128)S(1)}, f32[128]{0:T(128)S(1)}) all-reduce(f32[128]{0:T(128)S(1)} %get-tuple-element.111, f32[128]{0:T(128)S(1)} %get-tuple-element.110), channel_id=1, replica_groups=mesh['context'=4,'mirror'=2,'tensor'=4] {'tensor'}, use_global_device_ids=true, to_apply=%region_4.5 | all-reduce | flops 256 | bytes 2048 | tf_op jit(solution)/shard_map/psum | solution.py:68
  154.4 3.4 %fusion.45 = (bf16[128,2048]{0,1:T(8,128)(2,1)}, bf16[128,2048]{0,1:T(8,128)(2,1)}, bf16[128,2048]{0,1:T(8,128)(2,1)}) fusion(bf16[128,2048]{0,1:T(8,128)(2,1)} %copy.65, f32[128]{0:T(128)S(1)} %get-tuple-element.139, f32[128,16,128]{2,1,0:T(8,128)} %copy-done.1, f32[128,16,128]{0,2,1:T(8,128)} %copy-done.2, f32[2048]{0:T(1024)S(1)} %copy-done.20, ...), kind=kLoop, calls=%fused_computation.55 | loop fusion | flops 3407872 | bytes 4203520 | tf_op jit(solution)/shard_map/convert_element_type | solution.py:129
  157.7 3.8 %collective-permute-start.2 = (bf16[128,2048]{0,1:T(8,128)(2,1)}, bf16[128,2048]{0,1:T(8,128)(2,1)}, u32[]{:S(2)}, u32[]{:S(2)}) collective-permute-start(bf16[128,2048]{0,1:T(8,128)(2,1)} %get-tuple-element.134), channel_id=1, source_target_pairs={{0,4},{4,8},{8,12},{12,16},{16,20},{20,24},{24,28},{1,5},{5,9},{9,... | collective-permute-start | bytes 1572872 | tf_op jit(solution)/shard_map/ppermute | solution.py:14
  161.5 3.5 %collective-permute-start.1 = (bf16[128,2048]{0,1:T(8,128)(2,1)}, bf16[128,2048]{0,1:T(8,128)(2,1)}, u32[]{:S(2)}, u32[]{:S(2)}) collective-permute-start(bf16[128,2048]{0,1:T(8,128)(2,1)} %get-tuple-element.134), channel_id=1, source_target_pairs={{0,8},{4,12},{8,16},{12,20},{16,24},{20,28},{1,9},{5,13},{9,17},{1... | collective-permute-start | bytes 1572872 | tf_op jit(solution)/shard_map/ppermute | solution.py:14
  165.0 1.9 collective-permute-start.9
  166.9 67.7 %while.13 = (s32[]{:T(128)}, f32[4,32,128]{2,1,0:T(8,128)}, bf16[4,128,32,16]{1,3,2,0:T(8,128)(2,1)}, bf16[4,256,32,16]{1,3,2,0:T(8,128)(2,1)}, s32[256]{0:T(256...) while((s32[]{:T(128)}, f32[4,32,128]{2,1,0:T(8,128)}, bf16[4,128,32,16]{1,3,2,0:T(8,128)(2,1)}, ...), condition=%wide.region_14.15_spmd.clone, body=%wide.region_12.14_spmd.clone.sunk | while | flops 35188736 | bytes 32246372 | solution.py:168
  167.0 1.8 convolution_multiply_fusion.2
  168.8 2.4 copy.103
  171.2 2.2 pad.33
  173.5 8.0 %reshape.319 = f32[32,128,257]{2,1,0:T(8,128)} reshape(f32[32,32896]{1,0:T(8,128)} %pad.33) | data formatting | bytes 8421376 | tf_op jit(solution)/shard_map/while/body/eval_jaxpr/reshape | solution.py:159
  181.4 1.7 slice_reduce_fusion.2
  183.9 1.8 convolution_multiply_fusion.2
  185.7 2.4 copy.103
  188.1 2.2 pad.33
  190.4 8.0 %reshape.319 = f32[32,128,257]{2,1,0:T(8,128)} reshape(f32[32,32896]{1,0:T(8,128)} %pad.33) | data formatting | bytes 8421376 | tf_op jit(solution)/shard_map/while/body/eval_jaxpr/reshape | solution.py:159
  198.3 1.7 slice_reduce_fusion.2
  200.8 1.8 convolution_multiply_fusion.2
  202.6 2.4 copy.103
  205.1 2.2 pad.33
  207.3 8.0 %reshape.319 = f32[32,128,257]{2,1,0:T(8,128)} reshape(f32[32,32896]{1,0:T(8,128)} %pad.33) | data formatting | bytes 8421376 | tf_op jit(solution)/shard_map/while/body/eval_jaxpr/reshape | solution.py:159
  215.3 1.7 slice_reduce_fusion.2
  217.8 1.8 convolution_multiply_fusion.2
  219.5 2.4 copy.103
  222.0 2.2 pad.33
  224.2 8.0 %reshape.319 = f32[32,128,257]{2,1,0:T(8,128)} reshape(f32[32,32896]{1,0:T(8,128)} %pad.33) | data formatting | bytes 8421376 | tf_op jit(solution)/shard_map/while/body/eval_jaxpr/reshape | solution.py:159
  232.2 1.7 slice_reduce_fusion.2
  234.6 2.0 copy.88
  236.7 1.4 maximum_maximum_fusion.1
  238.1 6.8 %fusion.8 = f32[128,16,128]{2,1,0:T(8,128)} fusion(bf16[256,128,16]{0,2,1:T(8,128)(2,1)S(1)} %bitcast.175, bf16[128,128,256]{2,1,0:T(8,128)(2,1)} %copy.84, bf16[128,256]{1,0:T(8,128)(2,1)S(1)} %get-tuple-element.137), kind=kOutput, calls=%fused_computation.11 | convolution fusion | flops 138412032 | bytes 10551296 | tf_op jit(solution)/shard_map/gtu,ugc->tgc/dot_general | solution.py:138
  244.9 1.6 pad_maximum_fusion
  247.7 2.3 fusion.72
  250.0 6.6 %convolution_bitcast_fusion.1 = f32[384,16,128]{0,2,1:T(8,128)} fusion(bf16[128,16,128]{0,2,1:T(8,128)(2,1)} %bitcast.177, f32[16,384,128]{2,1,0:T(8,128)} %fusion.72, f32[16,384,128]{2,1,0:T(8,128)S(1)} %get-tuple-element.142, f32[16,128]{1,0:T(8,128)S(1)} %log_add_fusion, pred[128,384]{0,1:T(8,128)(4,1)S(1)} %fusion.54), kind=kOutput, calls=%fused_computation.32 | convolution fusion | flops 209979776 | bytes 10018816 | tf_op jit(solution)/shard_map/htu,thd->uhd/dot_general | solution.py:107
  256.6 3.4 %fusion.70 = (f32[128,16,128]{0,2,1:T(8,128)}, f32[128,16,128]{0,2,1:T(8,128)}) fusion(f32[384,16,128]{0,2,1:T(8,128)} %convolution_bitcast_fusion.1), kind=kLoop, calls=%fused_computation.99 | loop fusion | bytes 4194304 | tf_op jit(solution)/shard_map/slice | solution.py:116
  261.2 2.1 collective-permute-start.5
  264.6 2.0 copy.89
  266.6 2.0 copy.90
  268.7 3.0 convolution_convert_fusion
  271.6 2.0 copy.85
  273.7 6.2 %fusion.44 = bf16[16,128,128]{2,1,0:T(8,128)(2,1)} fusion(bf16[384,16,128]{0,2,1:T(8,128)(2,1)} %bitcast.172, f32[16,384,128]{2,1,0:T(8,128)} %fusion.72, f32[16,384,128]{2,1,0:T(8,128)S(1)} %get-tuple-element.142, f32[16,128]{1,0:T(8,128)S(1)} %log_add_fusion, pred[128,384]{0,1:T(8,128)(4,1)S(1)} %fusion.54), kind=kOutput, calls=%fused_computation.54 | convolution fusion | flops 210241920 | bytes 8445952 | tf_op jit(solution)/shard_map/htu,uhd->thd/dot_general | solution.py:102
  279.9 2.0 copy.86
  282.0 5.4 %collective-permute-done.6 = f32[128,16,128]{0,2,1:T(8,128)} collective-permute-done((f32[128,16,128]{0,2,1:T(8,128)}, f32[128,16,128]{0,2,1:T(8,128)}, u32[]{:S(2)}, u32[]{:S(2)}) %collective-permute-start.6) | collective-permute-done | bytes 1048608 | tf_op jit(solution)/shard_map/ppermute | solution.py:14
  287.4 11.5 %collective-permute-done.5 = f32[128,16,128]{0,2,1:T(8,128)} collective-permute-done((f32[128,16,128]{0,2,1:T(8,128)}, f32[128,16,128]{0,2,1:T(8,128)}, u32[]{:S(2)}, u32[]{:S(2)}) %collective-permute-start.5) | collective-permute-done | bytes 1048608 | tf_op jit(solution)/shard_map/ppermute | solution.py:14
  298.9 2.0 fusion.51
  301.9 1.5 copy.114
  (104 shorter events, 19.0 us)
Async XLA Ops:
  7.2 17.0 %copy-start.19 = (bf16[128,128]{1,0:T(8,128)(2,1)S(1)}, bf16[128,128]{1,0:T(8,128)(2,1)}, u32[]{:S(2)}) copy-start(bf16[128,128]{1,0:T(8,128)(2,1)} %param.14) | copy-start | bytes 98308
  7.2 17.2 %copy-start.16 = (bf16[128,2048]{1,0:T(8,128)(2,1)S(1)}, bf16[128,2048]{1,0:T(8,128)(2,1)}, u32[]{:S(2)}) copy-start(bf16[128,2048]{1,0:T(8,128)(2,1)} %param.11) | copy-start | bytes 1572868
  7.2 294.8 %all-reduce.6.cloned.1.call-start = ((), (), s32[]{:S(2)}) async-start(), calls=%async_computation | async-start | bytes 131072 | tf_op jit(solution)/shard_map/psum | solution.py:169
  8.6 16.8 %copy-start.17 = (bf16[128,2048]{1,0:T(8,128)(2,1)S(1)}, bf16[128,2048]{1,0:T(8,128)(2,1)}, u32[]{:S(2)}) copy-start(bf16[128,2048]{1,0:T(8,128)(2,1)} %param.18) | copy-start | bytes 1572868
  8.6 94.4 %collective-permute-start.4 = (bf16[128,2048]{0,1:T(8,128)(2,1)S(1)}, bf16[128,2048]{0,1:T(8,128)(2,1)}, u32[]{:S(2)}, u32[]{:S(2)}) collective-permute-start(bf16[128,2048]{0,1:T(8,128)(2,1)S(1)} %copy.70), channel_id=1, source_target_pairs={{0,4},{4,8},{8,12},{12,16},{16,20},{20,24},{24,28},{1,5},{5,9},{9,... | collective-permute-start | bytes 1572872 | tf_op jit(solution)/shard_map/ppermute | solution.py:14
  13.3 89.6 %collective-permute-start.3 = (bf16[128,2048]{0,1:T(8,128)(2,1)S(1)}, bf16[128,2048]{0,1:T(8,128)(2,1)}, u32[]{:S(2)}, u32[]{:S(2)}) collective-permute-start(bf16[128,2048]{0,1:T(8,128)(2,1)S(1)} %copy.70), channel_id=1, source_target_pairs={{0,8},{4,12},{8,16},{12,20},{16,24},{20,28},{1,9},{5,13},{9,17},{1... | collective-permute-start | bytes 1572872 | tf_op jit(solution)/shard_map/ppermute | solution.py:14
  18.7 9.1 %copy-start.8 = (bf16[128,2048]{0,1:T(8,128)(2,1)}, bf16[128,2048]{0,1:T(8,128)(2,1)S(1)}, u32[]{:S(2)}) copy-start(bf16[128,2048]{0,1:T(8,128)(2,1)S(1)} %copy.67) | copy-start | bytes 1572868
  18.7 7.7 %copy-start.21 = (s32[4]{0:T(128)S(1)}, s32[4]{0:T(128)}, u32[]{:S(2)}) copy-start(s32[4]{0:T(128)} %param.19) | copy-start | bytes 52
  18.7 8.0 %copy-start.18 = (bf16[128,2048]{1,0:T(8,128)(2,1)S(1)}, bf16[128,2048]{1,0:T(8,128)(2,1)}, u32[]{:S(2)}) copy-start(bf16[128,2048]{1,0:T(8,128)(2,1)} %param.16) | copy-start | bytes 1572868
  20.2 12.1 %copy-start.10 = (bf16[128,2048]{0,1:T(8,128)(2,1)}, bf16[128,2048]{0,1:T(8,128)(2,1)S(1)}, u32[]{:S(2)}) copy-start(bf16[128,2048]{0,1:T(8,128)(2,1)S(1)} %copy.66) | copy-start | bytes 1572868
  20.4 0.8 copy-start.6
  22.2 89.8 %collective-permute-start = (bf16[127,2048]{0,1:T(8,128)(2,1)}, bf16[127,2048]{0,1:T(8,128)(2,1)}, u32[]{:S(2)}, u32[]{:S(2)}) collective-permute-start(bf16[127,2048]{0,1:T(8,128)(2,1)} %slice.48), channel_id=1, source_target_pairs={{0,4},{4,8},{8,12},{12,16},{16,20},{20,24},{24,28},{1,5},{5,9},{9,... | collective-permute-start | bytes 1560584 | tf_op jit(solution)/shard_map/ppermute | solution.py:14
  102.5 1.9 copy-start.15
  104.4 1.5 copy-start.4
  104.4 1.5 copy-start.12
  105.3 8.3 %slice-start = ((s8[8388608]{0:T(1024)(128)(4,1)}), s8[4194304]{0:T(1024)(128)(4,1)S(1)}, s32[]{:S(2)}) async-start(s8[8388608]{0:T(1024)(128)(4,1)} %bitcast.163), calls=%async_computation.1 | async-start | bytes 8388608
  106.0 7.6 %slice-start.1 = ((s8[8388608]{0:T(1024)(128)(4,1)}), s8[4194304]{0:T(1024)(128)(4,1)S(1)}, s32[]{:S(2)}) async-start(s8[8388608]{0:T(1024)(128)(4,1)} %bitcast.163), calls=%async_computation.2 | async-start | bytes 8388608
  106.8 5.2 %copy-start.7 = (bf16[128,2048]{0,1:T(8,128)(2,1)S(1)}, bf16[128,2048]{0,1:T(8,128)(2,1)}, u32[]{:S(2)}) copy-start(bf16[128,2048]{0,1:T(8,128)(2,1)} %copy-done.6) | copy-start | bytes 1572868
  107.0 25.5 %collective-permute-start.8 = (f32[128,16,128]{0,2,1:T(8,128)S(1)}, f32[128,16,128]{0,2,1:T(8,128)S(1)}, u32[]{:S(2)}, u32[]{:S(2)}) collective-permute-start(f32[128,16,128]{0,2,1:T(8,128)S(1)} %get-tuple-element.131), channel_id=1, source_target_pairs={{8,0},{12,4},{16,8},{20,12},{24,16},{28,20},{9,1},{13,5},{17,9},{2... | collective-permute-start | bytes 3145736 | tf_op jit(solution)/shard_map/ppermute | solution.py:14
  108.6 36.8 %collective-permute-start.7 = (f32[128,16,128]{0,2,1:T(8,128)S(1)}, f32[128,16,128]{0,2,1:T(8,128)S(1)}, u32[]{:S(2)}, u32[]{:S(2)}) collective-permute-start(f32[128,16,128]{0,2,1:T(8,128)S(1)} %get-tuple-element.130), channel_id=1, source_target_pairs={{4,0},{8,4},{12,8},{16,12},{20,16},{24,20},{28,24},{5,1},{9,5},{13... | collective-permute-start | bytes 3145736 | tf_op jit(solution)/shard_map/ppermute | solution.py:14
  113.5 2.3 copy-start
  115.8 30.1 %copy-start.1 = (f32[128,16,128]{2,1,0:T(8,128)}, f32[128,16,128]{2,1,0:T(8,128)S(1)}, u32[]{:S(2)}) copy-start(f32[128,16,128]{2,1,0:T(8,128)S(1)} %fusion.10) | copy-start | bytes 3145732
  115.8 29.7 %copy-start.5 = (bf16[128,2048]{0,1:T(8,128)(2,1)S(1)}, bf16[128,2048]{0,1:T(8,128)(2,1)}, u32[]{:S(2)}) copy-start(bf16[128,2048]{0,1:T(8,128)(2,1)} %copy.65) | copy-start | bytes 1572868
  115.9 29.7 %copy-start.20 = (f32[2048]{0:T(1024)S(1)}, f32[2048]{0:T(1024)}, u32[]{:S(2)}) copy-start(f32[2048]{0:T(1024)} %param.15) | copy-start | bytes 24580
  145.6 1.0 copy-start.2
  157.7 87.1 %collective-permute-start.2 = (bf16[128,2048]{0,1:T(8,128)(2,1)}, bf16[128,2048]{0,1:T(8,128)(2,1)}, u32[]{:S(2)}, u32[]{:S(2)}) collective-permute-start(bf16[128,2048]{0,1:T(8,128)(2,1)} %get-tuple-element.134), channel_id=1, source_target_pairs={{0,4},{4,8},{8,12},{12,16},{16,20},{20,24},{24,28},{1,5},{5,9},{9,... | collective-permute-start | bytes 1572872 | tf_op jit(solution)/shard_map/ppermute | solution.py:14
  161.5 83.4 %collective-permute-start.1 = (bf16[128,2048]{0,1:T(8,128)(2,1)}, bf16[128,2048]{0,1:T(8,128)(2,1)}, u32[]{:S(2)}, u32[]{:S(2)}) collective-permute-start(bf16[128,2048]{0,1:T(8,128)(2,1)} %get-tuple-element.134), channel_id=1, source_target_pairs={{0,8},{4,12},{8,16},{12,20},{16,24},{20,28},{1,9},{5,13},{9,17},{1... | collective-permute-start | bytes 1572872 | tf_op jit(solution)/shard_map/ppermute | solution.py:14
  165.0 71.7 %collective-permute-start.9 = (bf16[127,2048]{0,1:T(8,128)(2,1)}, bf16[127,2048]{0,1:T(8,128)(2,1)}, u32[]{:S(2)}, u32[]{:S(2)}) collective-permute-start(bf16[127,2048]{0,1:T(8,128)(2,1)} %bitcast.150), channel_id=1, source_target_pairs={{4,0},{8,4},{12,8},{16,12},{20,16},{24,20},{28,24},{5,1},{9,5},{13... | collective-permute-start | bytes 1560584 | tf_op jit(solution)/shard_map/ppermute | solution.py:14
  244.9 2.8 copy-start.13
  246.5 1.2 copy-start.3
  256.6 6.8 %copy-start.9 = (bf16[128,2048]{0,1:T(8,128)(2,1)S(1)}, bf16[128,2048]{0,1:T(8,128)(2,1)}, u32[]{:S(2)}) copy-start(bf16[128,2048]{0,1:T(8,128)(2,1)} %copy-done.8) | copy-start | bytes 1572868
  256.6 6.8 %copy-start.11 = (bf16[128,2048]{0,1:T(8,128)(2,1)S(1)}, bf16[128,2048]{0,1:T(8,128)(2,1)}, u32[]{:S(2)}) copy-start(bf16[128,2048]{0,1:T(8,128)(2,1)} %copy-done.10) | copy-start | bytes 1572868
  256.6 6.8 %copy-start.14 = (f32[128,16,128]{2,1,0:T(8,128)S(1)}, f32[128,16,128]{2,1,0:T(8,128)}, u32[]{:S(2)}) copy-start(f32[128,16,128]{2,1,0:T(8,128)} %fusion.8) | copy-start | bytes 3145732
  260.0 27.4 %collective-permute-start.6 = (f32[128,16,128]{0,2,1:T(8,128)}, f32[128,16,128]{0,2,1:T(8,128)}, u32[]{:S(2)}, u32[]{:S(2)}) collective-permute-start(f32[128,16,128]{0,2,1:T(8,128)} %get-tuple-element.129), channel_id=1, source_target_pairs={{8,0},{12,4},{16,8},{20,12},{24,16},{28,20},{9,1},{13,5},{17,9},{2... | collective-permute-start | bytes 3145736 | tf_op jit(solution)/shard_map/ppermute | solution.py:14
  261.2 37.6 %collective-permute-start.5 = (f32[128,16,128]{0,2,1:T(8,128)}, f32[128,16,128]{0,2,1:T(8,128)}, u32[]{:S(2)}, u32[]{:S(2)}) collective-permute-start(f32[128,16,128]{0,2,1:T(8,128)} %get-tuple-element.128), channel_id=1, source_target_pairs={{4,0},{8,4},{12,8},{16,12},{20,16},{24,20},{28,24},{5,1},{9,5},{13... | collective-permute-start | bytes 3145736 | tf_op jit(solution)/shard_map/ppermute | solution.py:14
Sparse Core Ops, SparseCore 0:
  236.8 49.8 all-reduce.5
where the time goes:
time: 313 us; the launch traced here: 310 us
  local copies, waits for them, and re-layouts  155 us (50%)
  waiting for transfers between devices  46.5 us (15%)
  matrix products  35.9 us (11%)
  starting transfers between devices  28.2 us (9%)
  other arithmetic  21.9 us (7%)
  between operations  14.5 us (5%)
  blocking collectives  7.77 us (2%)
    ppermute x10, waiting for transfers between devices, passed_along(): return lax.ppermute(block, axis, route)  46.5 us
    another operation x4, local copies, waits for them, and re-layouts, banded(): jnp.tile(band_table, (1, row_count + 1))[:, :row_count * col_count]  35.4 us
    reshape x4, local copies, waits for them, and re-layouts, filter_block(): flattened.reshape(block_size, tok_rows, pad_rows + 1)[:, :, :tap_count]  31.8 us
    ppermute x10, starting transfers between devices, passed_along(): return lax.ppermute(block, axis, route)  28.2 us
    reshape x2, local copies, waits for them, and re-layouts, banded(): return repeated.reshape(band_table.shape[0], row_count, col_count)  25 us
    unnamed x61, local copies, waits for them, and re-layouts  20.7 us
    slice x2, local copies, waits for them, and re-layouts, banded(): jnp.tile(band_table, (1, row_count + 1))[:, :row_count * col_count]  14.1 us
    while x4, local copies, waits for them, and re-layouts  9.72 us
  transfers between devices with their start and end apart: 11, of which 4 were waited for; matrix products, arithmetic and copies ran while one was open for 66% of the time, Pallas kernels for 0%

commit v1 on v0

v1 whole, which is shorter than its diff:
```python
import functools

import jax
import jax.numpy as jnp
from jax import lax
from jax.experimental import pallas as pl
from jax.experimental.pallas import tpu as pltpu
from jax.sharding import PartitionSpec as P

HEAD = 128
LANES = 128
D = 8192
REACH = 2
NEG = -1e30
MESH = pl.DeviceIdType.MESH
F32 = jnp.float32
BF16 = jnp.bfloat16

KV, K2, K1, Q2, Q1, D2, D1, L1, L2, V2, V1, E1, E2, GS = range(14)
FIXED = 14


def dot_nt(a, b):
    return lax.dot_general(a, b, (((1,), (1,)), ((), ())), preferred_element_type=F32)


def dot_nn(a, b):
    return lax.dot_general(a, b, (((1,), (0,)), ((), ())), preferred_element_type=F32)


def kernel(
    dims,
    hq, hk, hv, filt, filt_rev, gain, aq, ak, og, lens,
    out, gq, gk, ghq, ghk, ghv, gfilt,
    kvwin, gswin, kwin, vwin, qwin, dwin, lrow, erow, prob, prob_t,
    qbias, kbias, fmask, bmask, rmask, signal, gval, cols, stat_out, stat_in,
    gflat, gpart, gin, gsum, send, recv,
):
    contexts, mirrors, tensors = dims
    count = contexts * mirrors
    rows, channels = hq.shape
    groups, taps = filt.shape
    width = channels // groups
    per = LANES // width
    blocks = channels // LANES
    heads = channels // HEAD
    subs = rows // taps
    scale = HEAD ** (-0.5)
    ctx = lax.axis_index("context")
    mir = lax.axis_index("mirror")
    ten = lax.axis_index("tensor")
    me = ctx * mirrors + mir
    base = me * rows

    def token(index):
        index = lax.rem(index + 2 * count, count)
        return {"context": index // mirrors, "mirror": lax.rem(index, mirrors)}

    def peer(index):
        return {"tensor": lax.rem(index, tensors)}

    barrier = pltpu.get_barrier_semaphore()
    for d in range(1, count):
        pl.semaphore_signal(barrier, inc=1, device_id=token(me + d), device_id_type=MESH)
    for d in range(1, tensors):
        pl.semaphore_signal(barrier, inc=1, device_id=peer(ten + d), device_id_type=MESH)
    pl.semaphore_wait(barrier, count - 1 + tensors - 1)

    def copy(slot, src, dst, device):
        return pltpu.make_async_remote_copy(
            src_ref=src, dst_ref=dst, send_sem=send.at[slot], recv_sem=recv.at[slot],
            device_id=device, device_id_type=MESH,
        )

    first, last = ctx == 0, ctx == contexts - 1
    inner_lo, inner_hi = jnp.logical_not(first), jnp.logical_not(last)
    core0, core1 = mir == 0, mir == 1
    partner = token(me + 1 - 2 * mir)
    far, mid, near = pl.ds(0, rows), pl.ds(rows, rows), pl.ds(2 * rows, rows)

    own_tail = pl.ds(rows, taps)
    c_kv = copy(KV, kvwin.at[own_tail], kvwin.at[pl.ds(0, taps)], token(me + 1))
    c_gs = copy(GS, gswin.at[pl.ds(0, taps)], gswin.at[pl.ds(rows, taps)], token(me - 1))
    has_lo, has_hi = me > 0, me < count - 1

    def forward(slot2, slot1, win):
        c2 = copy(slot2, win.at[near], win.at[far], token(me + 2))
        c1_own = copy(slot1, win.at[near], win.at[mid], partner)
        c1_relay = copy(slot1, win.at[far], win.at[mid], partner)
        return c2, c1_own, c1_relay

    def backward(slot2, slot1, win):
        c2 = copy(slot2, win.at[far], win.at[near], token(me - 2))
        c1_own = copy(slot1, win.at[far], win.at[mid], partner)
        c1_relay = copy(slot1, win.at[near], win.at[mid], partner)
        return c2, c1_own, c1_relay

    k_cp = forward(K2, K1, kwin)
    v_cp = forward(V2, V1, vwin)
    q_cp = backward(Q2, Q1, qwin)
    d_cp = backward(D2, D1, dwin)

    def rows_back(slot1, slot2, ref):
        return (
            copy(slot1, ref.at[0], ref.at[1], token(me - 1)),
            copy(slot2, ref.at[0], ref.at[2], token(me - 2)),
        )

    l_cp = rows_back(L1, L2, lrow)
    e_cp = rows_back(E1, E2, erow)

    def when(cond, fn):
        pl.when(cond)(fn)

    def start_forward(cps):
        when(inner_hi, cps[0].start)
        when(core0, cps[1].start)

    def start_backward(cps):
        when(inner_lo, cps[0].start)
        when(core1, cps[1].start)

    def land_forward(cps):
        when(inner_lo, cps[0].wait_recv)
        when(jnp.logical_and(core1, inner_lo), cps[2].start)

    def land_backward(cps):
        when(inner_hi, cps[0].wait_recv)
        when(jnp.logical_and(core0, inner_hi), cps[2].start)

    def finish_forward(cps):
        when(jnp.logical_or(core1, inner_lo), cps[1].wait_recv)

    def finish_backward(cps):
        when(jnp.logical_or(core0, inner_hi), cps[1].wait_recv)

    def drain_forward(cps):
        when(inner_hi, cps[0].wait_send)
        when(core0, cps[1].wait_send)
        when(jnp.logical_and(core1, inner_lo), cps[2].wait_send)

    def drain_backward(cps):
        when(inner_lo, cps[0].wait_send)
        when(core1, cps[1].wait_send)
        when(jnp.logical_and(core0, inner_hi), cps[2].wait_send)

    qwin[far] = aq[...]
    start_backward(q_cp)
    kvwin[pl.ds(taps, rows)] = (hk[...].astype(F32) * hv[...].astype(F32)).astype(BF16)
    when(has_hi, c_kv.start)
    kwin[near] = ak[...]
    start_forward(k_cp)
    dwin[far] = og[...]
    start_backward(d_cp)

    def zero(ref, at):
        ref[at] = jnp.zeros((ref[at].shape), ref.dtype)

    when(me == 0, lambda: zero(kvwin, pl.ds(0, taps)))
    when(me == count - 1, lambda: zero(gswin, pl.ds(rows, taps)))
    when(first, lambda: zero(kwin, far))
    when(first, lambda: zero(vwin, far))
    when(me == 0, lambda: zero(kwin, mid))
    when(me == 0, lambda: zero(vwin, mid))
    when(last, lambda: zero(qwin, near))
    when(last, lambda: zero(dwin, near))
    when(me == count - 1, lambda: zero(qwin, mid))
    when(me == count - 1, lambda: zero(dwin, mid))
    when(me == count - 1, lambda: zero(lrow, 1))
    when(me == count - 1, lambda: zero(erow, 1))
    when(me >= count - 2, lambda: zero(lrow, 2))
    when(me >= count - 2, lambda: zero(erow, 2))

    ends = []
    total = jnp.int32(0)
    for i in range(lens.shape[0]):
        total = total + lens[i]
        ends.append(total)

    def doc(pos):
        return sum((pos >= e).astype(jnp.int32) for e in ends)

    def grid(shape, row0, col0):
        return (
            row0 + lax.broadcasted_iota(jnp.int32, shape, 0),
            col0 + lax.broadcasted_iota(jnp.int32, shape, 1),
        )

    t_pos, u_pos = grid((rows, 3 * rows), base, base - 2 * rows)
    ok = (u_pos >= 0) & (u_pos <= t_pos) & (t_pos - u_pos <= REACH * rows) & (doc(u_pos) == doc(t_pos))
    qbias[...] = jnp.where(ok, 0.0, NEG)
    u_pos, t_pos = grid((rows, 3 * rows), base, base)
    ok = (u_pos <= t_pos) & (t_pos - u_pos <= REACH * rows) & (doc(u_pos) == doc(t_pos))
    kbias[...] = jnp.where(ok, 0.0, NEG)
    for s in range(subs):
        at = pl.ds(s * taps, taps)
        t_pos, u_pos = grid((taps, 2 * taps), base + s * taps, base + (s - 1) * taps)
        ok = (u_pos >= 0) & (u_pos <= t_pos) & (t_pos - u_pos < taps) & (doc(u_pos) == doc(t_pos))
        fmask[at] = jnp.where(ok, 1.0, 0.0).astype(BF16)
        halves = []
        for i in range(2):
            t_pos, w_pos = grid((taps, taps), base + s * taps, 0)
            u_pos = base + (s - 1 + i) * taps + lax.rem(taps - w_pos, taps)
            ok = (u_pos >= 0) & (u_pos <= t_pos) & (t_pos - u_pos < taps) & (doc(u_pos) == doc(t_pos))
            halves.append(jnp.where(ok, 1.0, 0.0))
        rmask[at] = jnp.concatenate(halves, axis=1)
        t_pos, u_pos = grid((taps, 2 * taps), base + s * taps, base + s * taps)
        ok = (u_pos >= t_pos) & (u_pos - t_pos < taps) & (doc(u_pos) == doc(t_pos))
        bmask[at] = jnp.where(ok, 1.0, 0.0).astype(BF16)

    lane = lax.broadcasted_iota(jnp.int32, (taps, LANES), 1)

    def chan(b):
        return pl.ds(pl.multiple_of(b * LANES, LANES), LANES)

    def toeplitz(ref, b):
        made = []
        for i in range(per):
            row = jnp.broadcast_to(ref[pl.ds(b * per + i, 1), :], (taps, taps))
            made.append(pltpu.roll(row, 0, 1, stride=1, stride_axis=0).astype(BF16))
        return made

    def conv(bands, mask, window):
        mask_lo, mask_hi = mask[:, :taps], mask[:, taps:]
        stack = jnp.concatenate(
            [jnp.concatenate([band * mask_lo, band * mask_hi], axis=1) for band in bands], axis=0
        )
        every = dot_nn(stack, window)
        picked = every[:taps]
        for i in range(1, per):
            picked = jnp.where(lane >= i * width, every[i * taps : (i + 1) * taps], picked)
        return picked

    when(has_lo, c_kv.wait_recv)

    def signal_step(b, acc):
        at = chan(b)
        bands = toeplitz(filt_rev, b)
        parts = []
        for s in range(subs):
            here = pl.ds(s * taps, taps)
            made = conv(bands, fmask[here], kvwin[pl.ds(s * taps, 2 * taps), at])
            signal[here, at] = made
            mix = hq[here, at].astype(F32) * made
            parts.append(mix * mix)
        return acc + jnp.concatenate(parts, axis=0)

    squares = lax.fori_loop(0, blocks, signal_step, jnp.zeros((rows, LANES), F32))

    land_forward(k_cp)
    finish_forward(k_cp)
    col_lane = lax.broadcasted_iota(jnp.int32, (rows, LANES), 1)

    def lse_step(h, acc):
        at = chan(h)
        score = dot_nt(aq[:, at], kwin[:, at]) * scale + qbias[...]
        top = jnp.max(score, axis=1, keepdims=True)
        lse = top + jnp.log(jnp.sum(jnp.exp(score - top), axis=1, keepdims=True))
        prob[h] = jnp.exp(score - lse)
        return jnp.where(col_lane == h, lse, acc)

    cols[...] = lax.fori_loop(0, heads, lse_step, jnp.zeros((rows, LANES), F32))
    lrow[0] = jnp.transpose(cols[...])[:heads]
    when(me > 0, l_cp[0].start)
    when(me > 1, l_cp[1].start)

    land_backward(q_cp)
    land_backward(d_cp)
    finish_backward(q_cp)
    finish_backward(d_cp)
    when(me < count - 1, l_cp[0].wait_recv)
    when(me < count - 2, l_cp[1].wait_recv)

    def wide_row(ref, h):
        return jnp.concatenate([ref[j, pl.ds(h, 1), :] for j in range(3)], axis=1)

    def gval_step(h, acc):
        at = chan(h)
        score = dot_nt(ak[:, at], qwin[:, at]) * scale + kbias[...]
        p = jnp.exp(score - wide_row(lrow, h))
        prob_t[h] = p
        made = dot_nn(p.astype(BF16), dwin[:, at])
        gval[:, at] = made
        return acc + gain[:, at] * made * (hq[:, at].astype(F32) * signal[:, at])

    inner = lax.fori_loop(0, heads, gval_step, jnp.zeros((rows, LANES), F32))

    cols[...] = jnp.where(
        col_lane == 0,
        jnp.sum(squares, axis=1, keepdims=True),
        jnp.where(col_lane == 1, jnp.sum(inner, axis=1, keepdims=True), 0.0),
    )
    stat_out[...] = jnp.transpose(cols[...])[:8]
    stat_cp = [
        copy(FIXED + d - 1, stat_out, stat_in.at[d - 1], peer(ten + d)) for d in range(1, tensors)
    ]
    for c in stat_cp:
        c.start()
    for c in stat_cp:
        c.wait_recv()
    stats = stat_out[...]
    for d in range(1, tensors):
        stats = stats + stat_in[d - 1]
    stats = jnp.transpose(jnp.concatenate([stats, jnp.zeros((LANES - 8, rows), F32)], axis=0))
    inv = lax.rsqrt(stats[:, 0:1] / D + 1e-06)
    pull = stats[:, 1:2] * inv * inv / D

    def norm_step(b, carry):
        at = chan(b)
        gate = hq[:, at].astype(F32)
        made = signal[:, at]
        mix = gate * made
        gains = gain[:, at]
        vwin[near, at] = (mix * inv * gains).astype(BF16)
        grad_mix = inv * (gains * gval[:, at] - mix * pull)
        ghq[:, at] = (grad_mix * made).astype(BF16)
        gswin[pl.ds(0, rows), at] = (grad_mix * gate).astype(BF16)
        return carry

    lax.fori_loop(0, blocks, norm_step, 0)
    when(has_lo, c_gs.start)
    start_forward(v_cp)

    row_at, col_at = grid((taps, taps), 0, 0)
    turn = jnp.where(lax.rem(row_at + col_at, taps) == 0, 1.0, 0.0).astype(BF16)

    def filter_step(b, carry):
        at = chan(b)
        sums = [jnp.zeros((1, taps), F32) for _ in range(per)]
        for s in range(subs):
            grads = gswin[pl.ds(s * taps, taps), at]
            stack = jnp.concatenate(
                [
                    jnp.where((lane >= i * width) & (lane < (i + 1) * width), grads, jnp.zeros_like(grads))
                    for i in range(per)
                ],
                axis=0,
            )
            turned = jnp.concatenate(
                [
                    dot_nn(turn, kvwin[pl.ds((s + i) * taps, taps), at]).astype(BF16)
                    for i in range(2)
                ],
                axis=0,
            )
            every = dot_nt(stack, turned)
            mask = rmask[pl.ds(s * taps, taps)]
            for i in range(per):
                part = every[i * taps : (i + 1) * taps] * mask
                part = part[:, :taps] + part[:, taps:]
                part = pltpu.roll(part, 0, 1, stride=1, stride_axis=0)
                sums[i] = sums[i] + jnp.sum(part, axis=0, keepdims=True)
        gflat[pl.ds(pl.multiple_of(b * per, per), per), :] = jnp.concatenate(sums, axis=0)
        return carry

    lax.fori_loop(0, blocks, filter_step, 0)
    share = groups // count
    for i in range(count):
        gpart[i] = gflat[i * share : (i + 1) * share]
    at0 = FIXED + tensors - 1
    scatter = [
        copy(at0 + d - 1, gpart.at[lax.rem(me + d, count)], gin.at[d - 1], token(me + d))
        for d in range(1, count)
    ]
    for c in scatter:
        c.start()

    when(has_hi, c_gs.wait_recv)

    def back_step(b, carry):
        at = chan(b)
        bands = toeplitz(filt, b)
        for s in range(subs):
            here = pl.ds(s * taps, taps)
            made = conv(bands, bmask[here], gswin[pl.ds(s * taps, 2 * taps), at])
            ghk[here, at] = (made * hv[here, at].astype(F32)).astype(BF16)
            ghv[here, at] = (made * hk[here, at].astype(F32)).astype(BF16)
        return carry

    lax.fori_loop(0, blocks, back_step, 0)

    for c in scatter:
        c.wait_recv()
    mine = gpart[me]
    for d in range(1, count):
        mine = mine + gin[d - 1]
    gsum[me] = mine
    at1 = at0 + count - 1
    gather = [
        copy(at1 + d - 1, gsum.at[me], gsum.at[me], token(me + d)) for d in range(1, count)
    ]
    for c in gather:
        c.start()

    land_forward(v_cp)
    finish_forward(v_cp)

    def query_step(h, acc):
        at = chan(h)
        values = vwin[:, at]
        p = prob[h]
        grad_p = dot_nt(og[:, at], values)
        out[:, at] = dot_nn(p.astype(BF16), values).astype(BF16)
        delta = jnp.sum(p * grad_p, axis=1, keepdims=True)
        ds = (p * (grad_p - delta) * scale).astype(BF16)
        gq[:, at] = dot_nn(ds, kwin[:, at]).astype(BF16)
        return jnp.where(col_lane == h, delta, acc)

    cols[...] = lax.fori_loop(0, heads, query_step, jnp.zeros((rows, LANES), F32))
    erow[0] = jnp.transpose(cols[...])[:heads]
    when(me > 0, e_cp[0].start)
    when(me > 1, e_cp[1].start)

    for d in range(1, count):
        other = lax.rem(me - d + count, count)
        copy(at1 + d - 1, gsum.at[other], gsum.at[other], token(me + d)).wait_recv()
    for i in range(count):
        gfilt[i * share : (i + 1) * share] = gsum[i]

    when(me < count - 1, e_cp[0].wait_recv)
    when(me < count - 2, e_cp[1].wait_recv)

    def key_step(h, carry):
        at = chan(h)
        grad_p = dot_nt(vwin[near, at], dwin[:, at])
        ds = (prob_t[h] * (grad_p - wide_row(erow, h)) * scale).astype(BF16)
        gk[:, at] = dot_nn(ds, qwin[:, at]).astype(BF16)
        return carry

    lax.fori_loop(0, heads, key_step, 0)

    when(has_hi, c_kv.wait_send)
    when(has_lo, c_gs.wait_send)
    drain_forward(k_cp)
    drain_forward(v_cp)
    drain_backward(q_cp)
    drain_backward(d_cp)
    for cps in (l_cp, e_cp):
        when(me > 0, cps[0].wait_send)
        when(me > 1, cps[1].wait_send)
    for c in stat_cp + scatter + gather:
        c.wait_send()


def body(dims, hyena_q, hyena_k, hyena_v, filters, norm_gain, attn_q, attn_k, out_grad, doc_lengths):
    contexts, mirrors, tensors = dims
    count = contexts * mirrors
    rows, channels = hyena_q.shape
    groups, taps = filters.shape
    heads = channels // HEAD
    share = groups // count
    filt = filters.astype(F32)
    filt_rev = jnp.concatenate([filt[:, :1], filt[:, :0:-1]], axis=1)
    slots = FIXED + tensors - 1 + 2 * (count - 1)
    window = (3 * rows, channels)
    tile = jax.ShapeDtypeStruct((rows, channels), BF16)
    vmem = pl.BlockSpec(memory_space=pltpu.VMEM)
    results = pl.pallas_call(
        functools.partial(kernel, dims),
        out_shape=(tile,) * 6 + (jax.ShapeDtypeStruct((groups, taps), F32),),
        in_specs=[vmem] * 9 + [pl.BlockSpec(memory_space=pltpu.SMEM)],
        out_specs=(vmem,) * 7,
        scratch_shapes=[
            pltpu.VMEM((taps + rows, channels), BF16),
            pltpu.VMEM((taps + rows, channels), BF16),
            pltpu.VMEM(window, BF16),
            pltpu.VMEM(window, BF16),
            pltpu.VMEM(window, BF16),
            pltpu.VMEM(window, BF16),
            pltpu.VMEM((3, heads, rows), F32),
            pltpu.VMEM((3, heads, rows), F32),
            pltpu.VMEM((heads, rows, 3 * rows), F32),
            pltpu.VMEM((heads, rows, 3 * rows), F32),
            pltpu.VMEM((rows, 3 * rows), F32),
            pltpu.VMEM((rows, 3 * rows), F32),
            pltpu.VMEM((rows, 2 * taps), BF16),
            pltpu.VMEM((rows, 2 * taps), BF16),
            pltpu.VMEM((rows, 2 * taps), F32),
            pltpu.VMEM((rows, channels), F32),
            pltpu.VMEM((rows, channels), F32),
            pltpu.VMEM((rows, LANES), F32),
            pltpu.VMEM((8, rows), F32),
            pltpu.VMEM((tensors - 1, 8, rows), F32),
            pltpu.VMEM((groups, taps), F32),
            pltpu.VMEM((count, share, taps), F32),
            pltpu.VMEM((count - 1, share, taps), F32),
            pltpu.VMEM((count, share, taps), F32),
            pltpu.SemaphoreType.DMA((slots,)),
            pltpu.SemaphoreType.DMA((slots,)),
        ],
        compiler_params=pltpu.CompilerParams(
            collective_id=0, has_side_effects=True, vmem_limit_bytes=63 * 1024 * 1024
        ),
        name="hyena_attention",
    )(
        hyena_q, hyena_k, hyena_v, filt, filt_rev, norm_gain[None, :], attn_q, attn_k, out_grad,
        doc_lengths,
    )
    return results


def solution(mesh):
    dims = (mesh.shape["context"], mesh.shape["mirror"], mesh.shape["tensor"])
    tokens = P(("context", "mirror"), "tensor")
    return jax.shard_map(
        functools.partial(body, dims),
        mesh=mesh,
        in_specs=(tokens, tokens, tokens, P("tensor", None), P("tensor"), tokens, tokens, tokens, P()),
        out_specs=(tokens,) * 6 + (P("tensor", None),),
        check_vma=False,
    )
```

time: 313 us -> 91.6 us (0.29)
  local copies, waits for them, and re-layouts: 155 us -> 9.34 us
  Pallas kernels: 0 us -> 79 us
  waiting for transfers between devices: 46.5 us -> 0 us
  matrix products: 35.9 us -> 0 us
  starting transfers between devices: 28.2 us -> 0 us
  other arithmetic: 21.9 us -> 1.37 us
  between operations: 14.5 us -> 0.67 us
  blocking collectives: 7.77 us -> 0 us
    pallas_call x0 -> x1, Pallas kernels: none -> 79 us  [body(): pl.pallas_call(functools.partial(kernel, dims), out_shape=(tile,) * 6 + (...]
    reshape x8 -> x0, local copies, waits for them, and re-layouts: 58.8 us -> none  [the longest x4 31.8 us: filter_block(): flattened.reshape(block_size, tok_rows, pad_rows + 1)[:, :, :tap_count]]
    ppermute x10 -> x0, waiting for transfers between devices: 46.5 us -> none  [passed_along(): return lax.ppermute(block, axis, route)]
    dot_general x12 -> x0, matrix products: 35.9 us -> none  [the longest x4 7.11 us: filter_block(): jnp.einsum('tgc,ugc->gtu', grad_block, wide_block, preferred_element_type...]
    another operation x4 -> x0, local copies, waits for them, and re-layouts: 35.4 us -> none  [banded(): jnp.tile(band_table, (1, row_count + 1))[:, :row_count * col_count]]
    ppermute x10 -> x0, starting transfers between devices: 28.2 us -> none  [passed_along(): return lax.ppermute(block, axis, route)]
    slice x5 -> x2, local copies, waits for them, and re-layouts: 18.8 us -> 0.91 us  [body(): filt_rev = jnp.concatenate([filt[:, :1], filt[:, :0:-1]], axis=1)]
    unnamed x61 -> x21, local copies, waits for them, and re-layouts: 20.7 us -> 8.36 us
  transfers between devices with their start and end apart: 11 -> 0, of which waited for: 4 -> 0; matrix products, arithmetic and copies ran while one was open for 66% -> 0% of each run, Pallas kernels for 0% -> 0%
where the time goes in v1:
time: 91.6 us; the launch traced here: 90.3 us
  Pallas kernels  79 us (86%)
  local copies, waits for them, and re-layouts  9.34 us (10%)
  other arithmetic  1.37 us (1%)
    pallas_call x1, Pallas kernels, body(): pl.pallas_call(functools.partial(kernel, dims), out_shape=(tile,) * 6 + (...  79 us
    unnamed x21, local copies, waits for them, and re-layouts  8.36 us

profile of v1, /device:TPU:1, one launch (start us, length us, event | category | flops | bytes accessed | tf_op | source)
XLA Modules:
  0.0 90.3 jit_solution(4390971874548547754)
XLA Ops:
  0.6 0.0 copy-start
  0.6 0.8 slice.8
  1.5 0.0 copy-done
  1.5 0.1 slice.9
  1.6 0.1 rev.3
  1.6 0.7 pad_maximum_fusion.filt_rev
  2.4 0.6 convert_element_type.3.filt
  3.0 79.0 %hyena_attention.1 = (bf16[128,2048]{1,0:T(8,128)(2,1)}, bf16[128,2048]{1,0:T(8,128)(2,1)}, bf16[128,2048]{1,0:T(8,128)(2,1)}, bf16[128,2048]{1,0:T(8,128)(2,1)}...) custom-call(bf16[128,2048]{1,0:T(8,128)(2,1)} %hq.1, bf16[128,2048]{1,0:T(8,128)(2,1)} %hk.1, ...), custom_call_target="tpu_custom_call" | custom-call | tf_op jit(solution)/shard_map/hyena_attention/pallas_call | solution.py:458
  82.0 0.0 copy-start.5
  82.0 1.9 %copy.23 = bf16[128,2048]{1,0:T(8,128)(2,1)} copy(bf16[128,2048]{1,0:T(8,128)(2,1)} %get-tuple-element.14) | data formatting | bytes 1048576
  83.9 0.0 copy-done.5
  83.9 0.0 copy-start.4
  83.9 0.8 copy.24
  84.7 0.4 copy-done.4
  85.2 0.0 copy-start.3
  85.2 0.8 copy.25
  86.0 0.4 copy-done.3
  86.4 0.0 copy-start.2
  86.4 0.8 copy.26
  87.2 0.4 copy-done.2
  87.6 0.0 copy-start.1
  87.6 0.8 copy.27
  88.4 0.4 copy-done.1
  88.9 0.0 copy-start.6
  88.9 0.8 copy.28
  89.6 0.1 copy-done.6
  89.7 0.6 copy.29
Async XLA Ops:
  0.6 0.8 copy-start
  82.0 2.0 %copy-start.5 = (bf16[128,2048]{1,0:T(8,128)(2,1)S(1)}, bf16[128,2048]{1,0:T(8,128)(2,1)}, u32[]{:S(2)}) copy-start(bf16[128,2048]{1,0:T(8,128)(2,1)} %get-tuple-element.15) | copy-start | bytes 1572868
  83.9 1.2 %copy-start.4 = (bf16[128,2048]{1,0:T(8,128)(2,1)S(1)}, bf16[128,2048]{1,0:T(8,128)(2,1)}, u32[]{:S(2)}) copy-start(bf16[128,2048]{1,0:T(8,128)(2,1)} %get-tuple-element.16) | copy-start | bytes 1572868
  85.2 1.2 %copy-start.3 = (bf16[128,2048]{1,0:T(8,128)(2,1)S(1)}, bf16[128,2048]{1,0:T(8,128)(2,1)}, u32[]{:S(2)}) copy-start(bf16[128,2048]{1,0:T(8,128)(2,1)} %get-tuple-element.17) | copy-start | bytes 1572868
  86.4 1.2 %copy-start.2 = (bf16[128,2048]{1,0:T(8,128)(2,1)S(1)}, bf16[128,2048]{1,0:T(8,128)(2,1)}, u32[]{:S(2)}) copy-start(bf16[128,2048]{1,0:T(8,128)(2,1)} %get-tuple-element.18) | copy-start | bytes 1572868
  87.6 1.2 %copy-start.1 = (bf16[128,2048]{1,0:T(8,128)(2,1)S(1)}, bf16[128,2048]{1,0:T(8,128)(2,1)}, u32[]{:S(2)}) copy-start(bf16[128,2048]{1,0:T(8,128)(2,1)} %get-tuple-element.19) | copy-start | bytes 1572868
  88.9 0.9 copy-start.6
